TPU v7x, 32 devices: a whole 2x2x4 slice. The times are simulated.
32 devices in a mesh: img: 16 (over z, y, core), tile: 2 (over x).
Axes of the slice: x: 2, y: 2, z: 4, core: 2. Of those that a mesh axis runs over, the one named last changes fastest.
Arguments:
- indices: int32 [64, 16, 16], P('img', 'tile'), may hold values from 0 to 6287, as said below
- embed_table: bfloat16 [6288, 768], P('img'), may hold values from -6 to 6
- w_qkv: bfloat16 [768, 2304], P('img'), may hold values from -0.21875 to 0.21875
- bias_q: float32 [768], replicated, may hold values from -1.75 to 1.75
- bias_v: float32 [768], replicated, may hold values from -1.75 to 1.75
- w_out: bfloat16 [768, 768], P('img'), may hold values from -0.875 to 0.875
- bias_out: float32 [768], replicated, may hold values from -1.75 to 1.75
- gain_one: float32 [768], replicated, may hold values from 0.1 to 1.9
- shift_one: float32 [768], replicated, may hold values from -1.75 to 1.75
- gain_two: float32 [768], replicated, may hold values from 0.1 to 1.9
- shift_two: float32 [768], replicated, may hold values from -1.75 to 1.75
- w_up: bfloat16 [768, 3072], P('img'), may hold values from -0.21875 to 0.21875
- bias_up: float32 [3072], replicated, may hold values from -1.75 to 1.75
- w_down: bfloat16 [3072, 768], P('img'), may hold values from -0.109375 to 0.109375
- bias_down: float32 [768], replicated, may hold values from -1.75 to 1.75
- w_conv: bfloat16 [9, 768, 768], P(None, 'img'), may hold values from -0.078125 to 0.078125
- bias_conv: float32 [768], replicated, may hold values from -1.75 to 1.75
- d_pixels: bfloat16 [64, 16, 16, 768], P('img', 'tile'), may hold values from -6 to 6
Outputs:
- pixels: float32 [64, 16, 16, 768], P('img', 'tile')
- grad_embed: float32 [64, 16, 16, 768], P('img', 'tile')
- grad_w_qkv: float32 [768, 2304], P('img')
- grad_bias_q: float32 [768], replicated
- grad_bias_v: float32 [768], replicated
- grad_w_out: float32 [768, 768], P('img')
- grad_bias_out: float32 [768], replicated
- grad_gain_one: float32 [768], replicated
- grad_shift_one: float32 [768], replicated
- grad_gain_two: float32 [768], replicated
- grad_shift_two: float32 [768], replicated
- grad_w_up: float32 [768, 3072], P('img')
- grad_bias_up: float32 [3072], replicated
- grad_w_down: float32 [3072, 768], P('img')
- grad_bias_down: float32 [768], replicated
- grad_w_conv: float32 [9, 768, 768], P(None, 'img')
- grad_bias_conv: float32 [768], replicated
Inputs may be any that keep to these rules, and one draw needn't show every extreme that they name: `indices`: the patches of one device (4 images, 8 patch rows of each) take at most 64 ids from any one block of 393 consecutive ids, and on every device exactly 64 from one block, the same block on all devices.
All inputs are finite; a program needn't handle non-finite values.
Results may differ from a plain program's by a relative error of at most 0.013.
Values may be sent and summed in bfloat16 or wider, within the bound.
A program may use at most 320 MiB of HBM per device.

v0:
```python
import math

import jax
import jax.numpy as jnp
from jax import lax
from jax.sharding import PartitionSpec as P

HEADS = 12


EPS = 1e-06


def extended_2(block, sides, width):
    for axis, dim in sides:
        count = lax.axis_size(axis)
        forward = [(i, i + 1) for i in range(count - 1)]
        backward = [(target, source) for source, target in forward]
        low = lax.ppermute(
            lax.slice_in_dim(block, block.shape[dim] - width, None, axis=dim), axis, forward
        )
        high = lax.ppermute(lax.slice_in_dim(block, 0, width, axis=dim), axis, backward)
        block = jnp.concatenate([low, block, high], axis=dim)
    return block


def norm_rows(values, gain, shift):
    center = values - jnp.mean(values, axis=-1, keepdims=True)
    spread = jnp.mean(center * center, axis=-1, keepdims=True)
    return center * lax.rsqrt(spread + EPS) * gain + shift


def shards(
    indices,
    embed_table,
    w_qkv,
    bias_q,
    bias_v,
    w_out,
    bias_out,
    gain_one,
    shift_one,
    gain_two,
    shift_two,
    w_up,
    bias_up,
    w_down,
    bias_down,
    w_conv,
    bias_conv,
    d_pixels,
):
    n_images, half_rows, grid_cols = indices.shape
    vocab_rows, model_width = embed_table.shape
    n_img = lax.axis_size("img")
    local_tokens = half_rows * grid_cols
    all_tokens = n_images * local_tokens
    capacity = max(2, 2 * all_tokens // n_img)
    flat_ids = indices.reshape(all_tokens)
    owner_dev = flat_ids // vocab_rows
    within = flat_ids - owner_dev * vocab_rows
    hits = (owner_dev[:, None] == jnp.arange(n_img, dtype=jnp.int32)[None, :]).astype(jnp.int32)
    slot_rank = jnp.sum((jnp.cumsum(hits, axis=0) - hits) * hits, axis=1)
    slot_index = owner_dev * capacity + slot_rank
    requests = (
        jnp.zeros((n_img * capacity,), jnp.int32)
        .at[slot_index]
        .set(within)
        .reshape(n_img, capacity)
    )
    found = jnp.take(
        embed_table,
        lax.all_to_all(requests, "img", split_axis=0, concat_axis=0, tiled=True),
        axis=0,
    )
    answers = lax.all_to_all(found, "img", split_axis=0, concat_axis=0, tiled=True)
    embedded = jnp.take(answers.reshape(n_img * capacity, model_width), slot_index, axis=0)
    token_rows = embedded.astype(jnp.float32).reshape(n_images, local_tokens, model_width)
    full_qkv, full_out, full_up, full_down, full_conv = (
        lax.all_gather(w_qkv, "img", axis=0, tiled=True),
        lax.all_gather(w_out, "img", axis=0, tiled=True),
        lax.all_gather(w_up, "img", axis=0, tiled=True),
        lax.all_gather(w_down, "img", axis=0, tiled=True),
        lax.all_gather(w_conv, "img", axis=1, tiled=True),
    )
    normed_one, pull_one = jax.vjp(norm_rows, token_rows, gain_one, shift_one)
    normed_low = normed_one.astype(jnp.bfloat16)
    zeros_k = jnp.zeros_like(bias_q)
    joined = jnp.einsum("bte,ef->btf", normed_low, full_qkv, preferred_element_type=jnp.float32)
    joined = joined + jnp.concatenate([bias_q, zeros_k, bias_v])
    joined_low = joined.astype(jnp.bfloat16).reshape(n_images, local_tokens, 3, HEADS, -1)
    queries = joined_low[:, :, 0]
    own_keys = joined_low[:, :, 1]
    own_values = joined_low[:, :, 2]
    all_keys, all_values = (
        lax.all_gather(own_keys, "tile", axis=1, tiled=True),
        lax.all_gather(own_values, "tile", axis=1, tiled=True),
    )
    scale = 1.0 / math.sqrt(queries.shape[-1])
    scores = (
        jnp.einsum("bqhd,bkhd->bhqk", queries, all_keys, preferred_element_type=jnp.float32) * scale
    )
    row_max = jnp.max(scores, axis=-1, keepdims=True)
    shifted = jnp.exp(scores - row_max)
    row_total = jnp.sum(shifted, axis=-1, keepdims=True)
    log_total = row_max + jnp.log(row_total)
    probs_low = (shifted / row_total).astype(jnp.bfloat16)
    mixed = jnp.einsum("bhqk,bkhd->bqhd", probs_low, all_values, preferred_element_type=jnp.float32)
    mixed_low = mixed.reshape(n_images, local_tokens, model_width).astype(jnp.bfloat16)
    stream_one = token_rows + (
        jnp.einsum("bte,ef->btf", mixed_low, full_out, preferred_element_type=jnp.float32)
        + bias_out
    )
    normed_two, pull_two = jax.vjp(norm_rows, stream_one, gain_two, shift_two)
    normed_two_low = normed_two.astype(jnp.bfloat16)
    hidden = (
        jnp.einsum("bte,em->btm", normed_two_low, full_up, preferred_element_type=jnp.float32)
        + bias_up
    )
    activated, pull_act = jax.vjp(jax.nn.gelu, hidden)
    activated_low = activated.astype(jnp.bfloat16)
    stream_two = stream_one + (
        jnp.einsum("btm,me->bte", activated_low, full_down, preferred_element_type=jnp.float32)
        + bias_down
    )
    surface = stream_two.astype(jnp.bfloat16).reshape(n_images, half_rows, grid_cols, model_width)
    extended = extended_2(surface, (("tile", 1),), 1)
    padded = jnp.pad(extended, ((0, 0), (0, 0), (1, 1), (0, 0)))
    pixels = bias_conv
    for row_off in range(3):
        for col_off in range(3):
            window = padded[:, row_off : row_off + half_rows, col_off : col_off + grid_cols]
            pixels = pixels + jnp.einsum(
                "brce,ef->brcf",
                window,
                full_conv[3 * row_off + col_off],
                preferred_element_type=jnp.float32,
            )
    back_qkv, back_out, back_up, back_down, back_conv = (
        lax.all_gather(w_qkv, "img", axis=0, tiled=True),
        lax.all_gather(w_out, "img", axis=0, tiled=True),
        lax.all_gather(w_up, "img", axis=0, tiled=True),
        lax.all_gather(w_down, "img", axis=0, tiled=True),
        lax.all_gather(w_conv, "img", axis=1, tiled=True),
    )
    conv_terms = []
    for row_off in range(3):
        for col_off in range(3):
            window = padded[:, row_off : row_off + half_rows, col_off : col_off + grid_cols]
            conv_terms.append(
                jnp.einsum("brce,brcf->ef", window, d_pixels, preferred_element_type=jnp.float32)
            )
    grad_w_conv = jnp.stack(conv_terms)
    grad_bias_conv = jnp.sum(d_pixels.astype(jnp.float32), axis=(0, 1, 2))
    cot_ext = extended_2(d_pixels, (("tile", 1),), 1)
    cot_pad = jnp.pad(cot_ext, ((0, 0), (0, 0), (1, 1), (0, 0)))
    d_surface = jnp.zeros((n_images, half_rows, grid_cols, model_width), jnp.float32)
    for row_off in range(3):
        for col_off in range(3):
            window = cot_pad[
                :, 2 - row_off : 2 - row_off + half_rows, 2 - col_off : 2 - col_off + grid_cols
            ]
            d_surface = d_surface + jnp.einsum(
                "brcf,ef->brce",
                window,
                back_conv[3 * row_off + col_off],
                preferred_element_type=jnp.float32,
            )
    d_stream_two = d_surface.reshape(n_images, local_tokens, model_width)
    branch_two = d_stream_two.astype(jnp.bfloat16)
    grad_w_down = jnp.einsum(
        "btm,bte->me", activated_low, branch_two, preferred_element_type=jnp.float32
    )
    grad_bias_down = jnp.sum(branch_two.astype(jnp.float32), axis=(0, 1))
    d_activated = jnp.einsum(
        "bte,me->btm", branch_two, back_down, preferred_element_type=jnp.float32
    )
    (d_hidden,) = pull_act(d_activated)
    d_hidden_low = d_hidden.astype(jnp.bfloat16)
    grad_w_up = jnp.einsum(
        "bte,btm->em", normed_two_low, d_hidden_low, preferred_element_type=jnp.float32
    )
    grad_bias_up = jnp.sum(d_hidden_low.astype(jnp.float32), axis=(0, 1))
    d_normed_two = jnp.einsum(
        "btm,em->bte", d_hidden_low, back_up, preferred_element_type=jnp.float32
    )
    d_from_two, grad_gain_two, grad_shift_two = pull_two(d_normed_two)
    d_stream_one = d_stream_two + d_from_two
    branch_one = d_stream_one.astype(jnp.bfloat16)
    grad_w_out = jnp.einsum(
        "bte,btf->ef", mixed_low, branch_one, preferred_element_type=jnp.float32
    )
    grad_bias_out = jnp.sum(branch_one.astype(jnp.float32), axis=(0, 1))
    d_mixed = jnp.einsum("btf,ef->bte", branch_one, back_out, preferred_element_type=jnp.float32)
    d_mixed = d_mixed.astype(jnp.bfloat16).reshape(n_images, local_tokens, HEADS, -1)
    scores_again = (
        jnp.einsum("bqhd,bkhd->bhqk", queries, all_keys, preferred_element_type=jnp.float32) * scale
    )
    probs_again = jnp.exp(scores_again - log_total)
    d_probs = jnp.einsum("bqhd,bkhd->bhqk", d_mixed, all_values, preferred_element_type=jnp.float32)
    inner = jnp.sum(probs_again * d_probs, axis=-1, keepdims=True)
    d_scores = (probs_again * (d_probs - inner)).astype(jnp.bfloat16)
    d_queries = (
        jnp.einsum("bhqk,bkhd->bqhd", d_scores, all_keys, preferred_element_type=jnp.float32)
        * scale
    )
    d_keys_all = (
        jnp.einsum("bhqk,bqhd->bkhd", d_scores, queries, preferred_element_type=jnp.float32) * scale
    )
    d_values_all = jnp.einsum(
        "bhqk,bqhd->bkhd",
        probs_again.astype(jnp.bfloat16),
        d_mixed,
        preferred_element_type=jnp.float32,
    )
    d_keys, d_values = (
        lax.psum_scatter(
            d_keys_all.astype(jnp.bfloat16), "tile", scatter_dimension=1, tiled=True
        ).astype(jnp.float32),
        lax.psum_scatter(
            d_values_all.astype(jnp.bfloat16), "tile", scatter_dimension=1, tiled=True
        ).astype(jnp.float32),
    )
    d_joined = jnp.stack([d_queries, d_keys, d_values], axis=2).astype(jnp.bfloat16)
    d_joined = d_joined.reshape(n_images, local_tokens, 3 * model_width)
    grad_w_qkv = jnp.einsum("bte,btf->ef", normed_low, d_joined, preferred_element_type=jnp.float32)
    joined_sums = jnp.sum(d_joined.astype(jnp.float32), axis=(0, 1))
    grad_bias_q = joined_sums[:model_width]
    grad_bias_v = joined_sums[2 * model_width :]
    d_normed_one = jnp.einsum("btf,ef->bte", d_joined, back_qkv, preferred_element_type=jnp.float32)
    d_from_one, grad_gain_one, grad_shift_one = pull_one(d_normed_one)
    grad_embed = (d_stream_one + d_from_one).reshape(n_images, half_rows, grid_cols, model_width)
    part_qkv, part_out, part_up, part_down, part_conv = (
        lax.psum_scatter(grad_w_qkv, "img", scatter_dimension=0, tiled=True),
        lax.psum_scatter(grad_w_out, "img", scatter_dimension=0, tiled=True),
        lax.psum_scatter(grad_w_up, "img", scatter_dimension=0, tiled=True),
        lax.psum_scatter(grad_w_down, "img", scatter_dimension=0, tiled=True),
        lax.psum_scatter(grad_w_conv, "img", scatter_dimension=1, tiled=True),
    )
    sum_qkv, sum_out, sum_up, sum_down, sum_conv = (
        lax.psum(part_qkv.astype(jnp.bfloat16), "tile").astype(jnp.float32),
        lax.psum(part_out.astype(jnp.bfloat16), "tile").astype(jnp.float32),
        lax.psum(part_up.astype(jnp.bfloat16), "tile").astype(jnp.float32),
        lax.psum(part_down.astype(jnp.bfloat16), "tile").astype(jnp.float32),
        lax.psum(part_conv.astype(jnp.bfloat16), "tile").astype(jnp.float32),
    )
    (
        sum_bias_q,
        sum_bias_v,
        sum_bias_out,
        sum_gain_one,
        sum_shift_one,
        sum_gain_two,
        sum_shift_two,
        sum_bias_up,
        sum_bias_down,
        sum_bias_conv,
    ) = lax.psum(
        (
            grad_bias_q,
            grad_bias_v,
            grad_bias_out,
            grad_gain_one,
            grad_shift_one,
            grad_gain_two,
            grad_shift_two,
            grad_bias_up,
            grad_bias_down,
            grad_bias_conv,
        ),
        ("img", "tile"),
    )
    return (
        pixels,
        grad_embed,
        sum_qkv,
        sum_bias_q,
        sum_bias_v,
        sum_out,
        sum_bias_out,
        sum_gain_one,
        sum_shift_one,
        sum_gain_two,
        sum_shift_two,
        sum_up,
        sum_bias_up,
        sum_down,
        sum_bias_down,
        sum_conv,
        sum_bias_conv,
    )


def solution(mesh):
    placed = (
        P("img", "tile", None),
        P("img", None),
        P("img", None),
        P(),
        P(),
        P("img", None),
        P(),
        P(),
        P(),
        P(),
        P(),
        P("img", None),
        P(),
        P("img", None),
        P(),
        P(None, "img", None),
        P(),
        P("img", "tile", None, None),
    )
    return jax.shard_map(
        shards,
        mesh=mesh,
        in_specs=placed,
        out_specs=(
            P("img", "tile", None, None),
            P("img", "tile", None, None),
            P("img", None),
            P(),
            P(),
            P("img", None),
            P(),
            P(),
            P(),
            P(),
            P(),
            P("img", None),
            P(),
            P("img", None),
            P(),
            P(None, "img", None),
            P(),
        ),
        check_vma=False,
    )
```

profile of v0, /device:TPU:0, one launch (start us, length us, event | category | flops | bytes accessed | tf_op | source)
XLA Modules:
  0.0 1167.7 jit_solution(15000323684026870304)
XLA Ops:
  14.6 13.6 %all_to_all.20 = s32[16,1,64]{2,1,0:T(1,128)S(1)} all-to-all(s32[16,1,64]{2,1,0:T(1,128)S(1)} %all_to_all.13), channel_id=1, replica_groups=mesh['img'=16,'tile'=2] {'img'}, dimensions={0} | all-to-all | bytes 8192 | tf_op jit(solution)/shard_map/all_to_all | solution.py:73
  37.7 45.9 %all-to-all-done.1 = bf16[16,64,768]{2,1,0:T(8,128)(2,1)S(1)} async-done(((bf16[16,64,768]{2,1,0:T(8,128)(2,1)}), bf16[16,64,768]{2,1,0:T(8,128)(2,1)S(1)}, u32[]{:S(2)}, u32[]{:S(2)}) %all-to-all-start.1) | async-done | bytes 1572896 | tf_op jit(solution)/shard_map/all_to_all | solution.py:76
  86.5 5.7 fusion.16
  102.4 4.6 collective-permute-start.2
  113.1 15.4 %all-gather.22.cloned.1.call-done = bf16[4,256,1,12,64]{1,4,3,0,2:T(8,128)(2,1)} async-done(((bf16[4,128,1,12,64]{1,4,3,0,2:T(8,128)(2,1)}), bf16[4,256,1,12,64]{1,4,3,0,2:T(8,128)(2,1)}) %all-gather.22.cloned.1.call-update) | async-done | bytes 1572880 | tf_op jit(solution)/shard_map/all_gather | solution.py:96
  136.4 23.6 %all-gather.20.cloned.1.call-done = bf16[4,256,1,12,64]{1,4,3,0,2:T(8,128)(2,1)} async-done(((bf16[4,128,1,12,64]{1,4,3,0,2:T(8,128)(2,1)}), bf16[4,256,1,12,64]{1,4,3,0,2:T(8,128)(2,1)}) %all-gather.20.cloned.1.call-update) | async-done | bytes 1572880 | tf_op jit(solution)/shard_map/all_gather | solution.py:97
  160.0 4.4 fusion.59
  164.4 36.1 %all-gather.12.cloned.1.call-done = bf16[768,768]{1,0:T(8,128)(2,1)} async-done(((bf16[48,768]{1,0:T(8,128)(2,1)}), bf16[768,768]{1,0:T(8,128)(2,1)}) %all-gather.12.cloned.1.call-update) | async-done | bytes 1179664 | tf_op jit(solution)/shard_map/all_gather | solution.py:81
  203.1 51.9 %all-gather.14.cloned.1.call-done = bf16[768,3072]{1,0:T(8,128)(2,1)} async-done(((bf16[48,3072]{1,0:T(8,128)(2,1)}), bf16[768,3072]{1,0:T(8,128)(2,1)}) %all-gather.14.cloned.1.call-update) | async-done | bytes 4718608 | tf_op jit(solution)/shard_map/all_gather | solution.py:82
  255.0 7.0 fusion.14
  262.0 82.4 %all-gather.18.cloned.1.call-done = bf16[9,768,768]{2,1,0:T(8,128)(2,1)} async-done(((bf16[9,48,768]{2,1,0:T(8,128)(2,1)}), bf16[9,768,768]{2,1,0:T(8,128)(2,1)}) %all-gather.18.cloned.1.call-update) | async-done | bytes 10616848 | tf_op jit(solution)/shard_map/all_gather | solution.py:84
  359.1 39.2 %all-gather.16.cloned.1.call-done = bf16[3072,768]{1,0:T(8,128)(2,1)} async-done(((bf16[192,768]{1,0:T(8,128)(2,1)}), bf16[3072,768]{1,0:T(8,128)(2,1)}) %all-gather.16.cloned.1.call-update) | async-done | bytes 4718608 | tf_op jit(solution)/shard_map/all_gather | solution.py:83
  398.3 9.8 convert_reduce_fusion
  408.1 7.1 multiply_reduce_fusion.2
  423.3 6.7 copy.96
  430.0 6.3 reshape.451
  437.7 5.6 multiply_reduce_fusion
  443.2 4.6 multiply_convert_fusion
  450.1 6.7 copy.94
  456.8 6.3 reshape.449
  468.1 4.5 multiply_bitcast_fusion
  478.1 11.4 reduce-scatter.22.cloned.1.call-done
  503.8 4.9 convolution_bitcast_fusion
  509.8 10.2 convolution_bitcast_fusion.1
  521.6 7.1 convolution_bitcast_fusion.2
  529.4 8.2 add_convert_fusion.1
  596.1 53.6 %reduce-scatter.12.cloned.1.call-done = f32[48,2304]{1,0:T(8,128)} async-done(((f32[768,2304]{1,0:T(8,128)}), f32[48,2304]{1,0:T(8,128)}) %reduce-scatter.12.cloned.1.call-update) | async-done | bytes 442384 | tf_op jit(solution)/shard_map/reduce_scatter | solution.py:234
  651.5 113.1 %reduce-scatter.18.cloned.1.call-done = f32[192,768]{1,0:T(8,128)} async-done(((f32[3072,768]{1,0:T(8,128)}), f32[192,768]{1,0:T(8,128)}) %reduce-scatter.18.cloned.1.call-update) | async-done | bytes 589840 | tf_op jit(solution)/shard_map/reduce_scatter | solution.py:237
  766.4 114.0 %reduce-scatter.16.cloned.1.call-done = f32[48,3072]{1,0:T(8,128)} async-done(((f32[768,3072]{1,0:T(8,128)}), f32[48,3072]{1,0:T(8,128)}) %reduce-scatter.16.cloned.1.call-update) | async-done | bytes 589840 | tf_op jit(solution)/shard_map/reduce_scatter | solution.py:236
  882.2 214.8 %reduce-scatter.20.cloned.1.call-done = f32[9,48,768]{2,1,0:T(8,128)} async-done(((f32[9,768,768]{2,1,0:T(8,128)}), f32[9,48,768]{2,1,0:T(8,128)}) %reduce-scatter.20.cloned.1.call-update) | async-done | bytes 1327120 | tf_op jit(solution)/shard_map/reduce_scatter | solution.py:238
  1099.2 7.2 add_add_fusion.4
  1109.2 41.3 %all-reduce.2 = (f32[768]{0:T(1024)}, f32[768]{0:T(1024)}, f32[768]{0:T(1024)}, f32[768]{0:T(1024)}, f32[768]{0:T(1024)}, /*index=5*/f32[768]{0:T(1024)}, f32[76...) all-reduce(f32[768]{0:T(1024)S(1)} %slice.179, ...), channel_id=1, replica_groups=mesh['img'=16,'tile'=2] {'img','tile'}, use_global_device_ids=true, to_apply=%region_20.21 | all-reduce | flops 9984 | bytes 79872 | tf_op jit(solution)/shard_map/psum | solution.py:258
  (254 shorter events, 179.6 us)
Async XLA Ops:
  7.2 79.3 %all-gather.10.cloned.1.call-start = ((), (), s32[]{:S(2)}) async-start(), calls=%async_computation.9 | async-start | bytes 3760128 | tf_op jit(solution)/shard_map/all_gather | solution.py:80
  33.7 49.9 %all-to-all-start.1 = ((bf16[16,64,768]{2,1,0:T(8,128)(2,1)}), bf16[16,64,768]{2,1,0:T(8,128)(2,1)S(1)}, u32[]{:S(2)}, u32[]{:S(2)}) async-start(bf16[16,64,768]{2,1,0:T(8,128)(2,1)} %broadcast_select_fusion), calls=%async_computation.1 | async-start | bytes 3145728 | tf_op jit(solution)/shard_map/all_to_all | solution.py:76
  37.6 91.0 %all-gather.22.cloned.1.call-start = ((), (), s32[]{:S(2)}) async-start(), calls=%async_computation.20 | async-start | bytes 2359296 | tf_op jit(solution)/shard_map/all_gather | solution.py:96
  96.8 63.1 %all-gather.20.cloned.1.call-start = ((), (), s32[]{:S(2)}) async-start(), calls=%async_computation.19 | async-start | bytes 2359296 | tf_op jit(solution)/shard_map/all_gather | solution.py:97
  97.6 102.9 %all-gather.12.cloned.1.call-start = ((), (), s32[]{:S(2)}) async-start(), calls=%async_computation.10 | async-start | bytes 1253376 | tf_op jit(solution)/shard_map/all_gather | solution.py:81
  98.1 156.8 %all-gather.14.cloned.1.call-start = ((), (), s32[]{:S(2)}) async-start(), calls=%async_computation.11 | async-start | bytes 5013504 | tf_op jit(solution)/shard_map/all_gather | solution.py:82
  98.7 245.7 %all-gather.18.cloned.1.call-start = ((), (), s32[]{:S(2)}) async-start(), calls=%async_computation.13 | async-start | bytes 11280384 | tf_op jit(solution)/shard_map/all_gather | solution.py:84
  99.3 299.0 %all-gather.16.cloned.1.call-start = ((), (), s32[]{:S(2)}) async-start(), calls=%async_computation.12 | async-start | bytes 5013504 | tf_op jit(solution)/shard_map/all_gather | solution.py:83
  100.0 372.6 %reduce-scatter.24.cloned.1.call-start = ((), (), s32[]{:S(2)}) async-start(), calls=%async_computation.22 | async-start | bytes 2359296
  101.1 7.4 collective-permute-start.3
  102.4 7.8 collective-permute-start.2
  136.4 64.1 %copy-start.38 = (f32[768]{0:T(1024)S(1)}, f32[768]{0:T(1024)}, u32[]{:S(2)}) copy-start(f32[768]{0:T(1024)} %param.24) | copy-start | bytes 9220
  164.4 38.3 %copy-start.16 = (bf16[4,12,64,128]{3,2,1,0:T(8,128)(2,1)}, bf16[4,12,64,128]{3,2,1,0:T(8,128)(2,1)S(1)}, u32[]{:S(2)}) copy-start(bf16[4,12,64,128]{3,2,1,0:T(8,128)(2,1)S(1)} %fusion.59) | copy-start | bytes 2359300
  202.7 59.3 %copy-start.8 = (f32[4,128,768]{2,1,0:T(8,128)}, f32[4,128,768]{2,1,0:T(8,128)S(1)}, u32[]{:S(2)}) copy-start(f32[4,128,768]{2,1,0:T(8,128)S(1)} %get-tuple-element.64) | copy-start | bytes 4718596
  202.7 52.3 %copy-start.45 = (f32[768]{0:T(1024)S(1)}, f32[768]{0:T(1024)}, u32[]{:S(2)}) copy-start(f32[768]{0:T(1024)} %param.27) | copy-start | bytes 9220
  202.7 52.3 %copy-start.48 = (f32[768]{0:T(1024)S(1)}, f32[768]{0:T(1024)}, u32[]{:S(2)}) copy-start(f32[768]{0:T(1024)} %param.28) | copy-start | bytes 9220
  203.1 141.4 %copy-start.13 = (bf16[4,8,16,768]{3,2,1,0:T(8,128)(2,1)S(1)}, bf16[4,8,16,768]{3,2,1,0:T(8,128)(2,1)}, u32[]{:S(2)}) copy-start(bf16[4,8,16,768]{3,2,1,0:T(8,128)(2,1)} %param.35) | copy-start | bytes 2359300
  358.1 57.8 %copy-start.4 = (f32[4,8,16,768]{3,2,1,0:T(8,128)}, f32[4,8,16,768]{3,2,1,0:T(8,128)S(1)}, u32[]{:S(2)}) copy-start(f32[4,8,16,768]{3,2,1,0:T(8,128)S(1)} %add_add_fusion.3) | copy-start | bytes 4718596
  358.1 40.1 %copy-start.47 = (f32[3072]{0:T(1024)S(1)}, f32[3072]{0:T(1024)}, u32[]{:S(2)}) copy-start(f32[3072]{0:T(1024)} %param.30) | copy-start | bytes 36868
  359.1 49.0 %copy-start.24 = (bf16[4,128,768]{2,1,0:T(8,128)(2,1)}, bf16[4,128,768]{2,1,0:T(8,128)(2,1)S(1)}, u32[]{:S(2)}) copy-start(bf16[4,128,768]{2,1,0:T(8,128)(2,1)S(1)} %get-tuple-element.50) | copy-start | bytes 2359300
  436.3 53.2 %reduce-scatter.22.cloned.1.call-start = ((), (), s32[]{:S(2)}) async-start(), calls=%async_computation.21 | async-start | bytes 2359296
  463.1 131.4 %reduce-scatter.14.cloned.1.call-start = ((), (), s32[]{:S(2)}) async-start(), calls=%async_computation.15 | async-start | bytes 2506752 | tf_op jit(solution)/shard_map/reduce_scatter | solution.py:235
  466.7 183.0 %reduce-scatter.12.cloned.1.call-start = ((), (), s32[]{:S(2)}) async-start(), calls=%async_computation.14 | async-start | bytes 7520256 | tf_op jit(solution)/shard_map/reduce_scatter | solution.py:234
  508.7 255.9 %reduce-scatter.18.cloned.1.call-start = ((), (), s32[]{:S(2)}) async-start(), calls=%async_computation.17 | async-start | bytes 10027008 | tf_op jit(solution)/shard_map/reduce_scatter | solution.py:237
  520.1 360.3 %reduce-scatter.16.cloned.1.call-start = ((), (), s32[]{:S(2)}) async-start(), calls=%async_computation.16 | async-start | bytes 10027008 | tf_op jit(solution)/shard_map/reduce_scatter | solution.py:236
  528.7 568.2 %reduce-scatter.20.cloned.1.call-start = ((), (), s32[]{:S(2)}) async-start(), calls=%async_computation.18 | async-start | bytes 22560768 | tf_op jit(solution)/shard_map/reduce_scatter | solution.py:238
  537.6 4.6 collective-permute-start
  540.0 6.5 collective-permute-start.1
  567.5 586.1 %all-reduce.6.cloned.1.call-start = ((), (), s32[]{:S(2)}) async-start(), calls=%async_computation.23 | async-start | bytes 3096576 | tf_op jit(solution)/shard_map/psum | solution.py:241
  882.2 217.0 %copy-start.40 = (f32[768]{0:T(1024)S(1)}, f32[768]{0:T(1024)}, u32[]{:S(2)}) copy-start(f32[768]{0:T(1024)} %param.34) | copy-start | bytes 9220
  1106.6 43.9 %copy-start.5 = (f32[4,8,16,768]{3,2,1,0:T(8,128)S(1)}, f32[4,8,16,768]{3,2,1,0:T(8,128)}, u32[]{:S(2)}) copy-start(f32[4,8,16,768]{3,2,1,0:T(8,128)} %copy-done.4) | copy-start | bytes 4718596
  1106.6 43.9 %copy-start.32 = (f32[4,128]{1,0:T(4,128)S(1)}, f32[4,128]{1,0:T(4,128)}, u32[]{:S(2)}) copy-start(f32[4,128]{1,0:T(4,128)} %copy-done.31) | copy-start | bytes 6148
  (39 other events, 204.5 us)
Sparse Core Ops, SparseCore 0:
  10.3 71.8 all-gather.9
  96.9 31.5 all-gather.21
  130.7 29.2 all-gather.19
  162.1 38.3 all-gather.11
  202.6 52.3 all-gather.13
  257.1 87.2 all-gather.17
  346.7 51.5 all-gather.15
  436.4 24.6 reduce-scatter.23
  463.4 26.0 reduce-scatter.21
  493.1 62.9 reduce-scatter.13
  560.6 89.0 reduce-scatter.11
  653.7 110.8 reduce-scatter.17
  769.2 111.0 reduce-scatter.15
  884.3 212.5 reduce-scatter.19
  1100.7 52.1 all-reduce.5
where the time goes:
time: 1180 us; the launch traced here: 1170 us
  waiting for transfers between devices  813 us (69%)
  matrix products  158 us (13%)
  local copies, waits for them, and re-layouts  67.2 us (6%)
  blocking collectives  54.9 us (5%)
  other arithmetic  44.2 us (4%)
  between operations  14.9 us (1%)
  starting transfers between devices  14.8 us (1%)
    reduce_scatter x1, waiting for transfers between devices, shards(): lax.psum_scatter(grad_w_conv, 'img', scatter_dimension=1, tiled=True)  215 us
    reduce_scatter x1, waiting for transfers between devices, shards(): lax.psum_scatter(grad_w_up, 'img', scatter_dimension=0, tiled=True)  114 us
    reduce_scatter x1, waiting for transfers between devices, shards(): lax.psum_scatter(grad_w_down, 'img', scatter_dimension=0, tiled=True)  113 us
    all_gather x1, waiting for transfers between devices, shards(): lax.all_gather(w_conv, 'img', axis=1, tiled=True)  82.4 us
    reduce_scatter x1, waiting for transfers between devices, shards(): lax.psum_scatter(grad_w_qkv, 'img', scatter_dimension=0, tiled=True)  53.6 us
    unnamed x111, local copies, waits for them, and re-layouts  52.2 us
    all_gather x1, waiting for transfers between devices, shards(): lax.all_gather(w_up, 'img', axis=0, tiled=True)  51.9 us
    all_to_all x1, waiting for transfers between devices, shards(): lax.all_to_all(found, 'img', split_axis=0, concat_axis=0, tiled=True)  45.9 us
  transfers between devices with their start and end apart: 20, of which 16 were waited for; matrix products, arithmetic and copies ran while one was open for 17% of the time, Pallas kernels for 0%

commit v1 on v0

--- a/solution.py
+++ b/solution.py
@@ -3,6 +3,8 @@
 import jax
 import jax.numpy as jnp
 from jax import lax
+from jax.experimental import pallas as pl
+from jax.experimental.pallas import tpu as pltpu
 from jax.sharding import PartitionSpec as P
 
 HEADS = 12
@@ -291,6 +293,658 @@
     )
 
 
+MESH = pl.DeviceIdType.MESH
+DIM = 768
+
+
+def unit_list():
+    return (
+        [("qkv", k) for k in range(3)]
+        + [("out", 0)]
+        + [("up", k) for k in range(4)]
+        + [("down", k) for k in range(4)]
+        + [("conv", t) for t in range(9)]
+    )
+
+
+def piece(refs, unit, where, columns):
+    name, k = unit
+    start, width = columns
+    ref = refs[name]
+    rows = pl.ds(0, 48)
+    if name == "conv":
+        where = (k,) + where
+    if name == "down":
+        rows = pl.ds(48 * k, 48)
+    if name in ("qkv", "up"):
+        start = start + DIM * k
+    return ref.at[where + (rows, pl.ds(aligned(start), width))]
+
+
+def aligned(start):
+    return start if isinstance(start, int) else pl.multiple_of(start, 128)
+
+
+def place():
+    img, tile = lax.axis_index("img"), lax.axis_index("tile")
+    return img // 4, lax.rem(img // 2, 2), lax.rem(img, 2), tile
+
+
+def device(z, y, c, x):
+    return (z * 4 + y * 2 + c, x)
+
+
+def greet(others):
+    barrier = pltpu.get_barrier_semaphore()
+    for other in others:
+        pl.semaphore_signal(barrier, inc=1, device_id=other, device_id_type=MESH)
+    pl.semaphore_wait(barrier, len(others))
+
+
+def neighbours():
+    z, y, c, x = place()
+    turn = [device(lax.rem(z + step, 4), y, c, x) for step in (1, 2, 3)]
+    return turn, device(z, 1 - y, c, x), device(z, y, c, 1 - x), device(z, y, 1 - c, x)
+
+
+class Gather:
+    def __init__(self, shards, full, send, recv, local):
+        self.shards, self.full, self.send, self.recv, self.local = shards, full, send, recv, local
+        z, y, c, x = place()
+        self.z, self.y, self.c, self.x = z, y, c, x
+        self.turn, self.dev_y, self.dev_x, self.dev_c = neighbours()
+        self.one = (0, 256)
+        self.mine = (256 + 256 * x, 256)
+        self.theirs = (512 - 256 * x, 256)
+
+    def copy(self, u, slot, src, dst, dev):
+        return pltpu.make_async_remote_copy(
+            src_ref=src,
+            dst_ref=dst,
+            send_sem=self.send.at[u, slot],
+            recv_sem=self.recv.at[u, slot],
+            device_id=dev,
+            device_id_type=MESH,
+        )
+
+    def at(self, u, where, columns):
+        return piece(self.full, UNITS[u], where, columns)
+
+    def hop(self, u, slot, where, columns, dev):
+        ref = self.at(u, where, columns)
+        return self.copy(u, slot, ref, ref, dev)
+
+    def own(self, u):
+        here = (self.z, self.y, self.c)
+        return [
+            pltpu.make_async_copy(
+                piece(self.shards, UNITS[u], (), columns),
+                self.at(u, here, columns),
+                self.local.at[u, n],
+            )
+            for n, columns in enumerate((self.one, self.mine))
+        ]
+
+    def along_z(self, u):
+        here = (self.z, self.y, self.c)
+        return [
+            self.copy(
+                u,
+                3 * n + step,
+                piece(self.shards, UNITS[u], (), columns),
+                self.at(u, here, columns),
+                self.turn[step],
+            )
+            for n, columns in enumerate((self.one, self.mine))
+            for step in range(3)
+        ]
+
+    def came_z(self, u):
+        out = []
+        for n, columns in enumerate((self.one, self.mine)):
+            for step in range(3):
+                ref = self.at(u, (lax.rem(self.z + 3 - step, 4), self.y, self.c), columns)
+                out.append(self.copy(u, 3 * n + step, ref, ref, self.turn[step]))
+        return out
+
+    def second(self, u, y, came=False):
+        c = 1 - self.c if came else self.c
+        y_out = 1 - self.y if came else self.y
+        all_z = slice(None)
+        return [
+            self.hop(u, 6, (all_z, y_out, self.c), self.one, self.dev_y),
+            self.hop(u, 7, (all_z, y_out, self.c), self.mine, self.dev_y),
+        ]
+
+    def to_x(self, u, slot, y, came=False):
+        columns = self.theirs if came else self.mine
+        return self.hop(u, slot, (slice(None), y, self.c), columns, self.dev_x)
+
+    def to_core(self, u, slot, y, columns, came=False):
+        c = 1 - self.c if came else self.c
+        return self.hop(u, slot, (slice(None), y, c), columns, self.dev_c)
+
+    def stage(self, u, step):
+        y = self.y
+        if step == 0:
+            for copy in self.along_z(u) + self.own(u):
+                copy.start()
+        if step == 1:
+            for copy in self.own(u):
+                copy.wait()
+            for copy in self.came_z(u):
+                copy.wait_recv()
+            for copy in self.second(u, y):
+                copy.start()
+            self.to_x(u, 8, y).start()
+            self.to_core(u, 10, y, self.one).start()
+            self.to_core(u, 11, y, self.mine).start()
+        if step == 2:
+            for copy in self.second(u, y, True):
+                copy.wait_recv()
+            self.to_x(u, 9, 1 - y).start()
+            self.to_core(u, 12, 1 - y, self.one).start()
+            self.to_core(u, 13, 1 - y, self.mine).start()
+        if step == 3:
+            self.to_x(u, 8, y, True).wait_recv()
+            self.to_x(u, 9, 1 - y, True).wait_recv()
+            self.to_core(u, 14, slice(None), self.theirs).start()
+        if step == 4:
+            self.to_core(u, 10, y, self.one, True).wait_recv()
+            self.to_core(u, 11, y, self.mine, True).wait_recv()
+            self.to_core(u, 12, 1 - y, self.one, True).wait_recv()
+            self.to_core(u, 13, 1 - y, self.mine, True).wait_recv()
+            self.to_core(u, 14, slice(None), self.theirs, True).wait_recv()
+        if step == 5:
+            for copy in self.along_z(u) + self.second(u, y):
+                copy.wait_send()
+            self.to_x(u, 8, y).wait_send()
+            self.to_x(u, 9, 1 - y).wait_send()
+            self.to_core(u, 10, y, self.one).wait_send()
+            self.to_core(u, 11, y, self.mine).wait_send()
+            self.to_core(u, 12, 1 - y, self.one).wait_send()
+            self.to_core(u, 13, 1 - y, self.mine).wait_send()
+            self.to_core(u, 14, slice(None), self.theirs).wait_send()
+
+
+UNITS = unit_list()
+NAMES = ("qkv", "out", "up", "down", "conv")
+
+
+def gather_kernel(*refs):
+    shards = dict(zip(NAMES, refs[:5]))
+    full = dict(zip(NAMES, refs[5:10]))
+    send, recv, local = refs[10:]
+    turn, dev_y, dev_x, dev_c = neighbours()
+    greet(turn + [dev_y, dev_x, dev_c])
+    gather = Gather(shards, full, send, recv, local)
+    count = len(UNITS)
+    for tick in range(count + 5):
+        for step in range(6):
+            if 0 <= tick - step < count:
+                gather.stage(tick - step, step)
+
+
+FULL = {
+    "qkv": (4, 2, 2, 48, 2304),
+    "out": (4, 2, 2, 48, 768),
+    "up": (4, 2, 2, 48, 3072),
+    "down": (4, 2, 2, 192, 768),
+    "conv": (9, 4, 2, 2, 48, 768),
+}
+
+
+def gather_weights(*shards):
+    count = len(UNITS)
+    return pl.pallas_call(
+        gather_kernel,
+        out_shape=[jax.ShapeDtypeStruct(FULL[name], jnp.bfloat16) for name in NAMES],
+        in_specs=[pl.BlockSpec(memory_space=pl.ANY)] * 5,
+        out_specs=[pl.BlockSpec(memory_space=pl.ANY)] * 5,
+        scratch_shapes=[
+            pltpu.SemaphoreType.DMA((count, 15)),
+            pltpu.SemaphoreType.DMA((count, 15)),
+            pltpu.SemaphoreType.DMA((count, 2)),
+        ],
+        compiler_params=pltpu.CompilerParams(collective_id=0, has_side_effects=True),
+        name="gather_weights",
+    )(*shards)
+
+
+class Scatter:
+    def __init__(self, partial, sums, buffers, send, recv, local, order):
+        self.partial, self.sums, self.order = partial, sums, order
+        self.own, self.core, self.ax, self.y_one, self.y_two, self.z_one, self.z_two, self.x_one, self.x_two = buffers
+        self.send, self.recv, self.local = send, recv, local
+        z, y, c, x = place()
+        self.z, self.y, self.c, self.x = z, y, c, x
+        self.turn, self.dev_y, self.dev_x, self.dev_c = neighbours()
+        self.one = (0, 512)
+        self.mine = (512 + 128 * x, 128)
+        self.theirs = (640 - 128 * x, 128)
+
+    def copy(self, n, slot, src, dst, dev):
+        return pltpu.make_async_remote_copy(
+            src_ref=src,
+            dst_ref=dst,
+            send_sem=self.send.at[n, slot],
+            recv_sem=self.recv.at[n, slot],
+            device_id=dev,
+            device_id_type=MESH,
+        )
+
+    def cols(self, columns):
+        return pl.ds(aligned(columns[0]), columns[1])
+
+    def sent(self, n, name, step=0):
+        y, y_cols = self.y, self.cols(self.one)
+        there = lax.rem(self.z + step + 1, 4)
+        if name == "core":
+            source = piece(self.partial, self.order[n], (slice(None), slice(None), 1 - self.c), (0, DIM))
+            return self.copy(n, 0, source, self.core.at[n], self.dev_c)
+        if name == "x":
+            return self.copy(n, 1, self.core.at[n, :, :, :, self.cols(self.theirs)], self.ax.at[n], self.dev_x)
+        if name == "y1":
+            return self.copy(n, 2, self.core.at[n, :, 1 - y, :, y_cols], self.y_one.at[n], self.dev_y)
+        if name == "y2":
+            return self.copy(n, 3, self.ax.at[n, :, 1 - y], self.y_two.at[n], self.dev_y)
+        if name == "z1":
+            return self.copy(n, 4 + step, self.y_one.at[n, there], self.z_one.at[n, step], self.turn[step])
+        if name == "z2":
+            return self.copy(n, 7 + step, self.y_two.at[n, there], self.z_two.at[n, step], self.turn[step])
+        if name == "x1":
+            return self.copy(n, 10, self.x_one.at[n, 0], self.x_one.at[n, 1], self.dev_x)
+        return self.copy(n, 11, self.x_two.at[n, 0], self.x_two.at[n, 1], self.dev_x)
+
+    def load(self, n):
+        u = self.order[n]
+        every = slice(None)
+        return pltpu.make_async_copy(
+            piece(self.partial, u, (every, every, self.c), (0, DIM)),
+            self.own.at[n % self.own.shape[0]],
+            self.local.at[n],
+        )
+
+    def stage(self, n, step):
+        f32, bf16 = jnp.float32, jnp.bfloat16
+        if step == 0:
+            self.sent(n, "core").start()
+            self.load(n).start()
+        if step == 1:
+            self.load(n).wait()
+            self.sent(n, "core").wait_recv()
+            mine = self.own.at[n % self.own.shape[0]]
+
+            @pl.loop(0, 4)
+            def _(i):
+                self.core[n, i] = (self.core[n, i].astype(f32) + mine[i].astype(f32)).astype(bf16)
+
+            self.sent(n, "x").start()
+            self.sent(n, "y1").start()
+        if step == 2:
+            self.sent(n, "x").wait_recv()
+            columns = self.cols(self.mine)
+
+            @pl.loop(0, 4)
+            def _(i):
+                self.ax[n, i] = (self.ax[n, i].astype(f32) + self.core[n, i, :, :, columns].astype(f32)).astype(bf16)
+
+            self.sent(n, "y2").start()
+            self.sent(n, "y1").wait_recv()
+            columns = self.cols(self.one)
+
+            @pl.loop(0, 4)
+            def _(i):
+                self.y_one[n, i] = (
+                    self.y_one[n, i].astype(f32) + self.core[n, i, self.y, :, columns].astype(f32)
+                ).astype(bf16)
+
+            for step_z in range(3):
+                self.sent(n, "z1", step_z).start()
+        if step == 3:
+            self.sent(n, "y2").wait_recv()
+
+            @pl.loop(0, 4)
+            def _(i):
+                self.y_two[n, i] = (self.y_two[n, i].astype(f32) + self.ax[n, i, self.y].astype(f32)).astype(bf16)
+
+            for step_z in range(3):
+                self.sent(n, "z2", step_z).start()
+            for step_z in range(3):
+                self.sent(n, "z1", step_z).wait_recv()
+            total = self.y_one[n, self.z].astype(f32)
+            for step_z in range(3):
+                total = total + self.z_one[n, step_z].astype(f32)
+            self.x_one[n, 0] = total.astype(bf16)
+            self.sent(n, "x1").start()
+        if step == 4:
+            for step_z in range(3):
+                self.sent(n, "z2", step_z).wait_recv()
+            total = self.y_two[n, self.z].astype(f32)
+            for step_z in range(3):
+                total = total + self.z_two[n, step_z].astype(f32)
+            self.x_two[n, 0] = total.astype(bf16)
+            self.sent(n, "x2").start()
+            self.sent(n, "x1").wait_recv()
+            self.out(n, self.one)[...] = self.x_one[n, 0].astype(f32) + self.x_one[n, 1].astype(f32)
+        if step == 5:
+            self.sent(n, "x2").wait_recv()
+            self.out(n, self.mine)[...] = self.x_two[n, 0].astype(f32)
+            self.out(n, self.theirs)[...] = self.x_two[n, 1].astype(f32)
+            for name in ("core", "x", "y1", "y2", "x1", "x2"):
+                self.sent(n, name).wait_send()
+            for name in ("z1", "z2"):
+                for step_z in range(3):
+                    self.sent(n, name, step_z).wait_send()
+
+    def out(self, n, columns):
+        return piece(self.sums, self.order[n], (), columns)
+
+
+ORDER = (
+    [("conv", t) for t in range(9)]
+    + [("down", k) for k in range(4)]
+    + [("up", k) for k in range(4)]
+    + [("out", 0)]
+    + [("qkv", k) for k in range(3)]
+)
+
+
+def scatter_scratch():
+    count = len(ORDER)
+    bf16 = jnp.bfloat16
+    return [
+        pltpu.VMEM((3, 4, 2, 48, DIM), bf16),
+        pltpu.VMEM((count, 4, 2, 48, DIM), bf16),
+        pltpu.VMEM((count, 4, 2, 48, 128), bf16),
+        pltpu.VMEM((count, 4, 48, 512), bf16),
+        pltpu.VMEM((count, 4, 48, 128), bf16),
+        pltpu.VMEM((count, 3, 48, 512), bf16),
+        pltpu.VMEM((count, 3, 48, 128), bf16),
+        pltpu.VMEM((count, 2, 48, 512), bf16),
+        pltpu.VMEM((count, 2, 48, 128), bf16),
+        pltpu.SemaphoreType.DMA((count, 12)),
+        pltpu.SemaphoreType.DMA((count, 12)),
+        pltpu.SemaphoreType.DMA((count,)),
+    ]
+
+
+def scatter_kernel(*refs):
+    partial = dict(zip(NAMES, refs[:5]))
+    sums = dict(zip(NAMES, refs[5:10]))
+    buffers, (send, recv, local) = refs[10:19], refs[19:]
+    turn, dev_y, dev_x, dev_c = neighbours()
+    greet(turn + [dev_y, dev_x, dev_c])
+    scatter = Scatter(partial, sums, buffers, send, recv, local, ORDER)
+    count = len(ORDER)
+    for tick in range(count + 5):
+        for step in range(6):
+            if 0 <= tick - step < count:
+                scatter.stage(tick - step, step)
+
+
+SUMS = {"qkv": (48, 2304), "out": (48, 768), "up": (48, 3072), "down": (192, 768), "conv": (9, 48, 768)}
+
+
+def scatter_grads(*partial):
+    return pl.pallas_call(
+        scatter_kernel,
+        out_shape=[jax.ShapeDtypeStruct(SUMS[name], jnp.float32) for name in NAMES],
+        in_specs=[pl.BlockSpec(memory_space=pl.ANY)] * 5,
+        out_specs=[pl.BlockSpec(memory_space=pltpu.VMEM)] * 5,
+        scratch_shapes=scatter_scratch(),
+        compiler_params=pltpu.CompilerParams(
+            collective_id=1, has_side_effects=True, vmem_limit_bytes=60 * 2**20
+        ),
+        name="scatter_grads",
+    )(*[part.reshape(FULL[name]) for name, part in zip(NAMES, partial)])
+
+
+def fast_shards(
+    indices,
+    embed_table,
+    w_qkv,
+    bias_q,
+    bias_v,
+    w_out,
+    bias_out,
+    gain_one,
+    shift_one,
+    gain_two,
+    shift_two,
+    w_up,
+    bias_up,
+    w_down,
+    bias_down,
+    w_conv,
+    bias_conv,
+    d_pixels,
+):
+    n_images, half_rows, grid_cols = indices.shape
+    vocab_rows, model_width = embed_table.shape
+    n_img = lax.axis_size("img")
+    local_tokens = half_rows * grid_cols
+    all_tokens = n_images * local_tokens
+    capacity = max(2, 2 * all_tokens // n_img)
+    flat_ids = indices.reshape(all_tokens)
+    owner_dev = flat_ids // vocab_rows
+    within = flat_ids - owner_dev * vocab_rows
+    hits = (owner_dev[:, None] == jnp.arange(n_img, dtype=jnp.int32)[None, :]).astype(jnp.int32)
+    slot_rank = jnp.sum((jnp.cumsum(hits, axis=0) - hits) * hits, axis=1)
+    slot_index = owner_dev * capacity + slot_rank
+    requests = (
+        jnp.zeros((n_img * capacity,), jnp.int32)
+        .at[slot_index]
+        .set(within)
+        .reshape(n_img, capacity)
+    )
+    found = jnp.take(
+        embed_table,
+        lax.all_to_all(requests, "img", split_axis=0, concat_axis=0, tiled=True),
+        axis=0,
+    )
+    answers = lax.all_to_all(found, "img", split_axis=0, concat_axis=0, tiled=True)
+    embedded = jnp.take(answers.reshape(n_img * capacity, model_width), slot_index, axis=0)
+    token_rows = embedded.astype(jnp.float32).reshape(n_images, local_tokens, model_width)
+    gathered = gather_weights(w_qkv, w_out, w_up, w_down, w_conv)
+    full_qkv, full_out, full_up, full_down, full_conv = (
+        gathered[0].reshape(768, 2304),
+        gathered[1].reshape(768, 768),
+        gathered[2].reshape(768, 3072),
+        gathered[3].reshape(3072, 768),
+        gathered[4].reshape(9, 768, 768),
+    )
+    back_qkv, back_out, back_up, back_down, back_conv = full_qkv, full_out, full_up, full_down, full_conv
+    normed_one, pull_one = jax.vjp(norm_rows, token_rows, gain_one, shift_one)
+    normed_low = normed_one.astype(jnp.bfloat16)
+    zeros_k = jnp.zeros_like(bias_q)
+    joined = jnp.einsum("bte,ef->btf", normed_low, full_qkv, preferred_element_type=jnp.float32)
+    joined = joined + jnp.concatenate([bias_q, zeros_k, bias_v])
+    joined_low = joined.astype(jnp.bfloat16).reshape(n_images, local_tokens, 3, HEADS, -1)
+    queries = joined_low[:, :, 0]
+    own_keys = joined_low[:, :, 1]
+    own_values = joined_low[:, :, 2]
+    all_keys, all_values = (
+        lax.all_gather(own_keys, "tile", axis=1, tiled=True),
+        lax.all_gather(own_values, "tile", axis=1, tiled=True),
+    )
+    scale = 1.0 / math.sqrt(queries.shape[-1])
+    scores = (
+        jnp.einsum("bqhd,bkhd->bhqk", queries, all_keys, preferred_element_type=jnp.float32) * scale
+    )
+    row_max = jnp.max(scores, axis=-1, keepdims=True)
+    shifted = jnp.exp(scores - row_max)
+    row_total = jnp.sum(shifted, axis=-1, keepdims=True)
+    log_total = row_max + jnp.log(row_total)
+    probs_low = (shifted / row_total).astype(jnp.bfloat16)
+    mixed = jnp.einsum("bhqk,bkhd->bqhd", probs_low, all_values, preferred_element_type=jnp.float32)
+    mixed_low = mixed.reshape(n_images, local_tokens, model_width).astype(jnp.bfloat16)
+    stream_one = token_rows + (
+        jnp.einsum("bte,ef->btf", mixed_low, full_out, preferred_element_type=jnp.float32)
+        + bias_out
+    )
+    normed_two, pull_two = jax.vjp(norm_rows, stream_one, gain_two, shift_two)
+    normed_two_low = normed_two.astype(jnp.bfloat16)
+    hidden = (
+        jnp.einsum("bte,em->btm", normed_two_low, full_up, preferred_element_type=jnp.float32)
+        + bias_up
+    )
+    activated, pull_act = jax.vjp(jax.nn.gelu, hidden)
+    activated_low = activated.astype(jnp.bfloat16)
+    stream_two = stream_one + (
+        jnp.einsum("btm,me->bte", activated_low, full_down, preferred_element_type=jnp.float32)
+        + bias_down
+    )
+    surface = stream_two.astype(jnp.bfloat16).reshape(n_images, half_rows, grid_cols, model_width)
+    extended = extended_2(surface, (("tile", 1),), 1)
+    padded = jnp.pad(extended, ((0, 0), (0, 0), (1, 1), (0, 0)))
+    pixels = bias_conv
+    for row_off in range(3):
+        for col_off in range(3):
+            window = padded[:, row_off : row_off + half_rows, col_off : col_off + grid_cols]
+            pixels = pixels + jnp.einsum(
+                "brce,ef->brcf",
+                window,
+                full_conv[3 * row_off + col_off],
+                preferred_element_type=jnp.float32,
+            )
+    conv_terms = []
+    for row_off in range(3):
+        for col_off in range(3):
+            window = padded[:, row_off : row_off + half_rows, col_off : col_off + grid_cols]
+            conv_terms.append(
+                jnp.einsum("brce,brcf->ef", window, d_pixels, preferred_element_type=jnp.float32)
+            )
+    grad_w_conv = jnp.stack(conv_terms)
+    grad_bias_conv = jnp.sum(d_pixels.astype(jnp.float32), axis=(0, 1, 2))
+    cot_ext = extended_2(d_pixels, (("tile", 1),), 1)
+    cot_pad = jnp.pad(cot_ext, ((0, 0), (0, 0), (1, 1), (0, 0)))
+    d_surface = jnp.zeros((n_images, half_rows, grid_cols, model_width), jnp.float32)
+    for row_off in range(3):
+        for col_off in range(3):
+            window = cot_pad[
+                :, 2 - row_off : 2 - row_off + half_rows, 2 - col_off : 2 - col_off + grid_cols
+            ]
+            d_surface = d_surface + jnp.einsum(
+                "brcf,ef->brce",
+                window,
+                back_conv[3 * row_off + col_off],
+                preferred_element_type=jnp.float32,
+            )
+    d_stream_two = d_surface.reshape(n_images, local_tokens, model_width)
+    branch_two = d_stream_two.astype(jnp.bfloat16)
+    grad_w_down = jnp.einsum(
+        "btm,bte->me", activated_low, branch_two, preferred_element_type=jnp.float32
+    )
+    grad_bias_down = jnp.sum(branch_two.astype(jnp.float32), axis=(0, 1))
+    d_activated = jnp.einsum(
+        "bte,me->btm", branch_two, back_down, preferred_element_type=jnp.float32
+    )
+    (d_hidden,) = pull_act(d_activated)
+    d_hidden_low = d_hidden.astype(jnp.bfloat16)
+    grad_w_up = jnp.einsum(
+        "bte,btm->em", normed_two_low, d_hidden_low, preferred_element_type=jnp.float32
+    )
+    grad_bias_up = jnp.sum(d_hidden_low.astype(jnp.float32), axis=(0, 1))
+    d_normed_two = jnp.einsum(
+        "btm,em->bte", d_hidden_low, back_up, preferred_element_type=jnp.float32
+    )
+    d_from_two, grad_gain_two, grad_shift_two = pull_two(d_normed_two)
+    d_stream_one = d_stream_two + d_from_two
+    branch_one = d_stream_one.astype(jnp.bfloat16)
+    grad_w_out = jnp.einsum(
+        "bte,btf->ef", mixed_low, branch_one, preferred_element_type=jnp.float32
+    )
+    grad_bias_out = jnp.sum(branch_one.astype(jnp.float32), axis=(0, 1))
+    d_mixed = jnp.einsum("btf,ef->bte", branch_one, back_out, preferred_element_type=jnp.float32)
+    d_mixed = d_mixed.astype(jnp.bfloat16).reshape(n_images, local_tokens, HEADS, -1)
+    scores_again = (
+        jnp.einsum("bqhd,bkhd->bhqk", queries, all_keys, preferred_element_type=jnp.float32) * scale
+    )
+    probs_again = jnp.exp(scores_again - log_total)
+    d_probs = jnp.einsum("bqhd,bkhd->bhqk", d_mixed, all_values, preferred_element_type=jnp.float32)
+    inner = jnp.sum(probs_again * d_probs, axis=-1, keepdims=True)
+    d_scores = (probs_again * (d_probs - inner)).astype(jnp.bfloat16)
+    d_queries = (
+        jnp.einsum("bhqk,bkhd->bqhd", d_scores, all_keys, preferred_element_type=jnp.float32)
+        * scale
+    )
+    d_keys_all = (
+        jnp.einsum("bhqk,bqhd->bkhd", d_scores, queries, preferred_element_type=jnp.float32) * scale
+    )
+    d_values_all = jnp.einsum(
+        "bhqk,bqhd->bkhd",
+        probs_again.astype(jnp.bfloat16),
+        d_mixed,
+        preferred_element_type=jnp.float32,
+    )
+    d_keys, d_values = (
+        lax.psum_scatter(
+            d_keys_all.astype(jnp.bfloat16), "tile", scatter_dimension=1, tiled=True
+        ).astype(jnp.float32),
+        lax.psum_scatter(
+            d_values_all.astype(jnp.bfloat16), "tile", scatter_dimension=1, tiled=True
+        ).astype(jnp.float32),
+    )
+    d_joined = jnp.stack([d_queries, d_keys, d_values], axis=2).astype(jnp.bfloat16)
+    d_joined = d_joined.reshape(n_images, local_tokens, 3 * model_width)
+    grad_w_qkv = jnp.einsum("bte,btf->ef", normed_low, d_joined, preferred_element_type=jnp.float32)
+    joined_sums = jnp.sum(d_joined.astype(jnp.float32), axis=(0, 1))
+    grad_bias_q = joined_sums[:model_width]
+    grad_bias_v = joined_sums[2 * model_width :]
+    d_normed_one = jnp.einsum("btf,ef->bte", d_joined, back_qkv, preferred_element_type=jnp.float32)
+    d_from_one, grad_gain_one, grad_shift_one = pull_one(d_normed_one)
+    grad_embed = (d_stream_one + d_from_one).reshape(n_images, half_rows, grid_cols, model_width)
+    sum_qkv, sum_out, sum_up, sum_down, sum_conv = scatter_grads(
+        *[grad.astype(jnp.bfloat16) for grad in (grad_w_qkv, grad_w_out, grad_w_up, grad_w_down, grad_w_conv)]
+    )
+    (
+        sum_bias_q,
+        sum_bias_v,
+        sum_bias_out,
+        sum_gain_one,
+        sum_shift_one,
+        sum_gain_two,
+        sum_shift_two,
+        sum_bias_up,
+        sum_bias_down,
+        sum_bias_conv,
+    ) = lax.psum(
+        (
+            grad_bias_q,
+            grad_bias_v,
+            grad_bias_out,
+            grad_gain_one,
+            grad_shift_one,
+            grad_gain_two,
+            grad_shift_two,
+            grad_bias_up,
+            grad_bias_down,
+            grad_bias_conv,
+        ),
+        ("img", "tile"),
+    )
+    return (
+        pixels,
+        grad_embed,
+        sum_qkv,
+        sum_bias_q,
+        sum_bias_v,
+        sum_out,
+        sum_bias_out,
+        sum_gain_one,
+        sum_shift_one,
+        sum_gain_two,
+        sum_shift_two,
+        sum_up,
+        sum_bias_up,
+        sum_down,
+        sum_bias_down,
+        sum_conv,
+        sum_bias_conv,
+    )
+
+
 def solution(mesh):
     placed = (
         P("img", "tile", None),
@@ -313,7 +967,7 @@
         P("img", "tile", None, None),
     )
     return jax.shard_map(
-        shards,
+        fast_shards if dict(mesh.shape) == {"img": 16, "tile": 2} else shards,
         mesh=mesh,
         in_specs=placed,
         out_specs=(

time: 1180 us -> 618 us (0.52)
  waiting for transfers between devices: 813 us -> 30.7 us
  Pallas kernels: 0 us -> 276 us
  matrix products: 158 us -> 111 us
  local copies, waits for them, and re-layouts: 67.2 us -> 88 us
  other arithmetic: 44.2 us -> 23.9 us
    reduce_scatter x5 -> x0, waiting for transfers between devices: 495 us -> none  [the longest x1 215 us: shards(): lax.psum_scatter(grad_w_conv, 'img', scatter_dimension=1, tiled=True)]
    pallas_call x0 -> x2, Pallas kernels: none -> 276 us  [the longest x1 143 us: gather_weights(): pl.pallas_call(gather_kernel, out_shape=[jax.ShapeDtypeStruct(FULL[name],...]
    all_gather x7 -> x2, waiting for transfers between devices: 249 us -> 30.6 us  [the longest x1 23 us: fast_shards(): lax.all_gather(own_values, 'tile', axis=1, tiled=True)]
    dot_general x45, matrix products: 158 us -> 111 us  [the longest x9 22.4 us: fast_shards(): jnp.einsum('brcf,ef->brce', window, back_conv[3 * row_off + col_off], pre...]
    all_to_all x1, waiting for transfers between devices: 45.9 us -> 0.01 us  [fast_shards(): lax.all_to_all(found, 'img', split_axis=0, concat_axis=0, tiled=True)]
    convert_element_type x13 -> x3, other arithmetic: 21.5 us -> 5.01 us  [the longest x1 4.59 us: fast_shards(): d_scores = (probs_again * (d_probs - inner)).astype(jnp.bfloat16)]
    unnamed x17 -> x6, waiting for transfers between devices: 15.2 us -> 0.09 us
    unnamed x111 -> x193, local copies, waits for them, and re-layouts: 52.2 us -> 62.6 us
  transfers between devices with their start and end apart: 20 -> 9, of which waited for: 16 -> 2; matrix products, arithmetic and copies ran while one was open for 17% -> 22% of each run, Pallas kernels for 0% -> 23%
where the time goes in v1:
time: 618 us; the launch traced here: 614 us
  Pallas kernels  276 us (45%)
  matrix products  111 us (18%)
  local copies, waits for them, and re-layouts  88 us (14%)
  blocking collectives  53.9 us (9%)
  waiting for transfers between devices  30.7 us (5%)
  other arithmetic  23.9 us (4%)
  starting transfers between devices  15.5 us (3%)
  between operations  15.2 us (2%)
    pallas_call x1, Pallas kernels, gather_weights(): pl.pallas_call(gather_kernel, out_shape=[jax.ShapeDtypeStruct(FULL[name],...  143 us
    pallas_call x1, Pallas kernels, scatter_grads(): pl.pallas_call(scatter_kernel, out_shape=[jax.ShapeDtypeStruct(SUMS[name]...  133 us
    unnamed x193, local copies, waits for them, and re-layouts  62.6 us
    psum x1, blocking collectives, fast_shards(): lax.psum((grad_bias_q, grad_bias_v, grad_bias_out, grad_gain_one, grad_sh...  40.4 us
    all_gather x1, waiting for transfers between devices, fast_shards(): lax.all_gather(own_values, 'tile', axis=1, tiled=True)  23 us
    dot_general x9, matrix products, fast_shards(): jnp.einsum('brcf,ef->brce', window, back_conv[3 * row_off + col_off], pre...  22.4 us
    all_to_all x1, blocking collectives, fast_shards(): lax.all_to_all(requests, 'img', split_axis=0, concat_axis=0, tiled=True)  13.6 us
  transfers between devices with their start and end apart: 9, of which 2 were waited for; matrix products, arithmetic and copies ran while one was open for 22% of the time, Pallas kernels for 23%

profile of v1, /device:TPU:0, one launch (start us, length us, event | category | flops | bytes accessed | tf_op | source)
XLA Modules:
  0.0 614.0 jit_solution(9914412472878349725)
XLA Ops:
  14.0 13.6 %all_to_all.20 = s32[16,1,64]{2,1,0:T(1,128)S(1)} all-to-all(s32[16,1,64]{2,1,0:T(1,128)S(1)} %all_to_all.13), channel_id=1, replica_groups=mesh['img'=16,'tile'=2] {'img'}, dimensions={0} | all-to-all | bytes 8192 | tf_op jit(solution)/shard_map/all_to_all | solution.py:743
  27.7 4.0 gather_fusion
  33.0 3.8 all-to-all-start.1
  37.0 3.4 collective-permute-start.2
  41.9 143.0 %gather_weights.1 = (bf16[4,2,2,48,2304]{4,3,2,1,0:T(8,128)(2,1)}, bf16[4,2,2,48,768]{4,3,2,1,0:T(8,128)(2,1)}, bf16[4,2,2,48,3072]{4,3,2,1,0:T(8,128)(2,1)}, bf...) custom-call(bf16[48,2304]{1,0:T(8,128)(2,1)} %refs_0_.1, bf16[48,768]{1,0:T(8,128)(2,1)} %refs_1_.1, ...), custom_call_target="tpu_custom_call" | custom-call | tf_op jit(solution)/shard_map/gather_weights/pallas_call | solution.py:499
  185.7 7.2 %fusion.133 = (bf16[1,4,2,2,48,768]{5,4,3,2,1,0:T(8,128)(2,1)}, bf16[1,4,2,2,48,768]{5,4,3,2,1,0:T(8,128)(2,1)S(1)}, bf16[1,4,2,2,48,768]{5,4,3,2,1,0:T(8,128)(2...) fusion(bf16[9,4,2,2,48,768]{5,4,3,2,1,0:T(8,128)(2,1)} %get-tup, ...), kind=kLoop, calls=%fused_computation.222 | loop fusion | bytes 21233664 | tf_op jit(solution)/shard_map/slice | solution.py:808
  204.0 5.4 fusion.8
  209.4 4.3 copy.60
  227.7 6.3 %fusion.32 = f32[4,8,16,768]{3,2,1,0:T(8,128)S(1)} fusion(f32[4,8,16,768]{3,2,1,0:T(8,128)} %fusion.65, f32[4,8,16,768]{3,2,1,0:T(8,128)} %fusion.73, f32[4,8,16,768]{3,2,1,0:T(8,128)} %fusion.75, f32[768,4,8,16]{0,3,2,1:T(8,128)} %fusion.139, f32[4,8,16,768]{3,2,1,0:T(8,128)} %fusion.77, f32[4,8,16,768]{3,2,1,0:T(8,128)} %fusion.79, ...), kind=kOutput, calls=%fused_computation.70 | convolution fusion | flops 607125504 | bytes 16121856 | tf_op jit(solution)/shard_map/brcf,ef->brce/dot_general | solution.py:828
  236.1 7.6 %all-gather.7.cloned.1.call-done = bf16[4,256,1,12,64]{1,4,3,0,2:T(8,128)(2,1)} async-done(((bf16[4,128,1,12,64]{1,4,3,0,2:T(8,128)(2,1)}), bf16[4,256,1,12,64]{1,4,3,0,2:T(8,128)(2,1)}) %all-gather.7.cloned.1.call-update) | async-done | bytes 1572880 | tf_op jit(solution)/shard_map/all_gather | solution.py:768
  243.7 3.0 multiply_reduce_fusion.1
  249.5 23.0 %all-gather.5.cloned.1.call-done = bf16[4,256,1,12,64]{1,4,3,0,2:T(8,128)(2,1)} async-done(((bf16[4,128,1,12,64]{1,4,3,0,2:T(8,128)(2,1)}), bf16[4,256,1,12,64]{1,4,3,0,2:T(8,128)(2,1)}) %all-gather.5.cloned.1.call-update) | async-done | bytes 1572880 | tf_op jit(solution)/shard_map/all_gather | solution.py:769
  272.5 4.5 fusion.55
  278.8 4.8 fusion.113
  283.7 8.6 %add_convert_fusion = bf16[4,128,768]{2,1,0:T(8,128)(2,1)S(1)} fusion(f32[4,128,768]{2,1,0:T(8,128)S(1)} %get-tuple-element.89, bf16[3072,768,1]{1,0,2:T(8,128)(2,1)} %bitcast.386, f32[768]{0:T(1024)S(1)} %copy-done.75, f32[4,128,3072]{2,1,0:T(8,128)S(1)} %fusion.113, f32[3072]{0:T(1024)S(1)} %copy-done.74), kind=kOutput, calls=%fused_computation.86 | convolution fusion | flops 2432827392 | bytes 13384704 | tf_op jit(solution)/shard_map/btm,me->bte/dot_general | solution.py:795
  294.5 5.0 collective-permute-start
  299.5 7.1 %convert_reduce_fusion = (f32[3072]{0:T(1024)}, bf16[4,128,3072]{2,1,0:T(8,128)(2,1)S(1)}) fusion(f32[4,128,3072]{2,1,0:T(8,128)S(1)} %fusion.113, f32[3072]{0:T(1024)S(1)} %copy-done.74, bf16[4,128,768]{2,1,0:T(8,128)(2,1)S(1)} %bitcast.376, bf16[3072,768,1]{1,0,2:T(8,128)(2,1)S(1)} %bitcast.389), kind=kOutput, calls=%fused_computation.15 | convolution fusion | flops 2452091904 | bytes 14966784 | tf_op jit(solution)/shard_map/bte,me->btm/dot_general | solution.py:840
  306.6 3.5 multiply_reduce_fusion.2
  314.0 4.1 fusion.44
  318.1 6.7 %copy.100 = bf16[4,256,12,64]{3,2,0,1:T(8,128)(2,1)} copy(bf16[4,256,12,64]{1,3,2,0:T(8,128)(2,1)S(1)} %fusion.44) | data formatting | bytes 3145728
  324.8 6.3 %reshape.553 = bf16[256,3072]{1,0:T(8,128)(2,1)} reshape(bf16[256,4,12,64]{3,2,1,0:T(8,128)(2,1)} %bitcast.317) | data formatting | bytes 3145728
  332.5 5.1 multiply_reduce_fusion
  337.6 4.6 multiply_convert_fusion
  344.4 6.7 %copy.98 = bf16[4,256,12,64]{3,2,0,1:T(8,128)(2,1)} copy(bf16[4,256,12,64]{1,3,2,0:T(8,128)(2,1)S(1)} %fusion.47) | data formatting | bytes 3145728
  351.1 6.4 %reshape.551 = bf16[256,3072]{1,0:T(8,128)(2,1)} reshape(bf16[256,4,12,64]{3,2,1,0:T(8,128)(2,1)} %bitcast.318) | data formatting | bytes 3145728
  361.3 4.9 bitcast_convert_fusion.1
  366.1 5.4 bitcast_convert_fusion
  373.0 4.0 fusion.58
  408.9 3.0 reshape.552
  417.6 3.9 bitcast_convert_fusion.2
  427.8 132.7 %scatter_grads.1 = (f32[48,2304]{1,0:T(8,128)}, f32[48,768]{1,0:T(8,128)}, f32[48,3072]{1,0:T(8,128)}, f32[192,768]{1,0:T(8,128)}, f32[9,48,768]{2,1,0:T(8,128)}) custom-call(bf16[4,2,2,48,2304]{4,3,2,1,0:T(8,128)(2,1)} %bitcast.339, bf16[4,2,2,48,768]{4,3,2,1,0:T(8,128)(2,1)} %bitcast.345, bf16[4,2,2,48,3072]{4,3,2,1,0:T(8,128)(2,1)} %bitcast.329, ...), custom_call_target="tpu_custom_call" | custom-call | tf_op jit(solution)/shard_map/scatter_grads/pallas_call | solution.py:690
  560.7 40.4 %all-reduce.2 = (f32[768]{0:T(1024)}, f32[768]{0:T(1024)}, f32[768]{0:T(1024)}, f32[768]{0:T(1024)}, f32[768]{0:T(1024)}, /*index=5*/f32[768]{0:T(1024)}, f32[76...) all-reduce(f32[768]{0:T(1024)S(1)} %slice.188, ...), channel_id=1, replica_groups=mesh['img'=16,'tile'=2] {'img','tile'}, use_global_device_ids=true, to_apply=%region_18.19 | all-reduce | flops 9984 | bytes 79872 | tf_op jit(solution)/shard_map/psum | solution.py:912
  (301 shorter events, 106.7 us)
Async XLA Ops:
  7.2 20.5 %copy-start = (bf16[393,768]{1,0:T(8,128)(2,1)S(1)}, bf16[393,768]{1,0:T(8,128)(2,1)}, u32[]{:S(2)}) copy-start(bf16[393,768]{1,0:T(8,128)(2,1)} %param.19) | copy-start | bytes 1810948
  33.0 166.1 %all-to-all-start.1 = ((bf16[16,64,768]{2,1,0:T(8,128)(2,1)}), bf16[16,64,768]{2,1,0:T(8,128)(2,1)S(1)}, u32[]{:S(2)}, u32[]{:S(2)}) async-start(bf16[16,64,768]{2,1,0:T(8,128)(2,1)} %broadcast_select_fusion), calls=%async_computation.1 | async-start | bytes 3145728 | tf_op jit(solution)/shard_map/all_to_all | solution.py:746
  36.9 148.0 %copy-start.70 = (f32[768]{0:T(1024)S(1)}, f32[768]{0:T(1024)}, u32[]{:S(2)}) copy-start(f32[768]{0:T(1024)} %param.22) | copy-start | bytes 9220
  36.9 148.0 %copy-start.71 = (f32[768]{0:T(1024)S(1)}, f32[768]{0:T(1024)}, u32[]{:S(2)}) copy-start(f32[768]{0:T(1024)} %param.21) | copy-start | bytes 9220
  36.9 206.8 %all-gather.7.cloned.1.call-start = ((), (), s32[]{:S(2)}) async-start(), calls=%async_computation.5 | async-start | bytes 2359296 | tf_op jit(solution)/shard_map/all_gather | solution.py:768
  37.0 158.2 %collective-permute-start.2 = (bf16[4,1,16,768]{3,2,1,0:T(8,128)(2,1)S(1)}, bf16[4,1,16,768]{3,2,1,0:T(8,128)(2,1)S(1)}, u32[]{:S(2)}, u32[]{:S(2)}) collective-permute-start(bf16[4,1,16,768]{3,2,1,0:T(8,128)(2,1)S(1)} %get-tuple-element.77), channel_id=1, source_target_pairs={{0,1},{2,3},{4,5},{6,7},{8,9},{10,11},{12,13},{14,15},{16,17},{18,... | collective-permute-start | bytes 294920 | tf_op jit(solution)/shard_map/ppermute | solution.py:21
  40.4 156.8 %collective-permute-start.3 = (bf16[4,1,16,768]{3,2,1,0:T(8,128)(2,1)S(1)}, bf16[4,1,16,768]{3,2,1,0:T(8,128)(2,1)S(1)}, u32[]{:S(2)}, u32[]{:S(2)}) collective-permute-start(bf16[4,1,16,768]{3,2,1,0:T(8,128)(2,1)S(1)} %get-tuple-element.76), channel_id=1, source_target_pairs={{1,0},{3,2},{5,4},{7,6},{9,8},{11,10},{13,12},{15,14},{17,16},{19,... | collective-permute-start | bytes 294920 | tf_op jit(solution)/shard_map/ppermute | solution.py:24
  185.7 91.3 %copy-start.63 = (pred[4,128]{1,0:T(4,128)(4,1)}, pred[4,128]{1,0:T(4,128)(4,1)S(1)}, u32[]{:S(2)}) copy-start(pred[4,128]{1,0:T(4,128)(4,1)S(1)} %compare_and_fusion.2) | copy-start | bytes 1540
  201.2 75.8 %copy-start.3 = (bf16[512,768]{1,0:T(8,128)(2,1)}, bf16[512,768]{1,0:T(8,128)(2,1)S(1)}, u32[]{:S(2)}) copy-start(bf16[512,768]{1,0:T(8,128)(2,1)S(1)} %gather_fusion.1) | copy-start | bytes 2359300
  216.4 56.0 %all-gather.5.cloned.1.call-start = ((), (), s32[]{:S(2)}) async-start(), calls=%async_computation.4 | async-start | bytes 2359296 | tf_op jit(solution)/shard_map/all_gather | solution.py:769
  217.4 8.2 %copy-start.21 = (bf16[4,10,18,768]{3,2,1,0:T(8,128)(2,1)}, bf16[4,10,18,768]{3,2,1,0:T(8,128)(2,1)S(1)}, u32[]{:S(2)}) copy-start(bf16[4,10,18,768]{3,2,1,0:T(8,128)(2,1)S(1)} %select_maximum_fusion) | copy-start | bytes 3317764
  227.6 176.4 %reduce-scatter.9.cloned.1.call-start = ((), (), s32[]{:S(2)}) async-start(), calls=%async_computation.7 | async-start | bytes 2359296
  234.0 76.7 %copy-start.6 = (f32[4,8,16,768]{3,2,1,0:T(8,128)}, f32[4,8,16,768]{3,2,1,0:T(8,128)S(1)}, u32[]{:S(2)}) copy-start(f32[4,8,16,768]{3,2,1,0:T(8,128)S(1)} %fusion.32) | copy-start | bytes 4718596
  249.4 27.6 %copy-start.66 = (f32[768]{0:T(1024)S(1)}, f32[768]{0:T(1024)}, u32[]{:S(2)}) copy-start(f32[768]{0:T(1024)} %param.24) | copy-start | bytes 9220
  278.0 32.1 %copy-start.9 = (f32[4,128,768]{2,1,0:T(8,128)}, f32[4,128,768]{2,1,0:T(8,128)S(1)}, u32[]{:S(2)}) copy-start(f32[4,128,768]{2,1,0:T(8,128)S(1)} %get-tuple-element.89) | copy-start | bytes 4718596
  278.8 20.7 %slice-start.2 = ((s8[4718592]{0:T(1024)(128)(4,1)}), s8[4194304]{0:T(1024)(128)(4,1)S(1)}, s32[]{:S(2)}) async-start(s8[4718592]{0:T(1024)(128)(4,1)} %bitcast.387), calls=%async_computation.10 | async-start | bytes 8388608
  283.6 15.8 %copy-start.77 = (f32[4,128,3072]{2,1,0:T(8,128)}, f32[4,128,3072]{2,1,0:T(8,128)S(1)}, u32[]{:S(2)}) copy-start(f32[4,128,3072]{2,1,0:T(8,128)S(1)} %fusion.113) | copy-start | bytes 18874372
  283.7 15.8 %copy-start.47 = (bf16[4,8,16,768]{3,2,1,0:T(8,128)(2,1)S(1)}, bf16[4,8,16,768]{3,2,1,0:T(8,128)(2,1)}, u32[]{:S(2)}) copy-start(bf16[4,8,16,768]{3,2,1,0:T(8,128)(2,1)} %get-tuple-element.55) | copy-start | bytes 2359300
  283.7 15.8 %slice-start.3 = ((s8[4718592]{0:T(1024)(128)(4,1)}), s8[524288]{0:T(1024)(128)(4,1)S(1)}, s32[]{:S(2)}) async-start(s8[4718592]{0:T(1024)(128)(4,1)} %bitcast.387), calls=%async_computation.11 | async-start | bytes 1048576
  283.7 22.9 %slice-start = ((s8[4718592]{0:T(1024)(128)(4,1)}), s8[4194304]{0:T(1024)(128)(4,1)S(1)}, s32[]{:S(2)}) async-start(s8[4718592]{0:T(1024)(128)(4,1)} %bitcast.383), calls=%async_computation.8 | async-start | bytes 8388608
  293.2 86.6 %collective-permute-start.1 = (bf16[4,1,16,768]{3,2,1,0:T(8,128)(2,1)S(1)}, bf16[4,1,16,768]{3,2,1,0:T(8,128)(2,1)S(1)}, u32[]{:S(2)}, u32[]{:S(2)}) collective-permute-start(bf16[4,1,16,768]{3,2,1,0:T(8,128)(2,1)S(1)} %get-tuple-element.79), channel_id=1, source_target_pairs={{1,0},{3,2},{5,4},{7,6},{9,8},{11,10},{13,12},{15,14},{17,16},{19,... | collective-permute-start | bytes 294920 | tf_op jit(solution)/shard_map/ppermute | solution.py:24
  294.5 85.3 %collective-permute-start = (bf16[4,1,16,768]{3,2,1,0:T(8,128)(2,1)S(1)}, bf16[4,1,16,768]{3,2,1,0:T(8,128)(2,1)S(1)}, u32[]{:S(2)}, u32[]{:S(2)}) collective-permute-start(bf16[4,1,16,768]{3,2,1,0:T(8,128)(2,1)S(1)} %get-tuple-element.78), channel_id=1, source_target_pairs={{0,1},{2,3},{4,5},{6,7},{8,9},{10,11},{12,13},{14,15},{16,17},{18,... | collective-permute-start | bytes 294920 | tf_op jit(solution)/shard_map/ppermute | solution.py:21
  299.5 7.1 %slice-start.1 = ((s8[4718592]{0:T(1024)(128)(4,1)}), s8[524288]{0:T(1024)(128)(4,1)S(1)}, s32[]{:S(2)}) async-start(s8[4718592]{0:T(1024)(128)(4,1)} %bitcast.383), calls=%async_computation.9 | async-start | bytes 1048576
  331.1 77.7 %reduce-scatter.7.cloned.1.call-start = ((), (), s32[]{:S(2)}) async-start(), calls=%async_computation.6 | async-start | bytes 2359296
  427.8 132.9 %copy-start.59 = (f32[768]{0:T(1024)S(1)}, f32[768]{0:T(1024)}, u32[]{:S(2)}) copy-start(f32[768]{0:T(1024)} %convert_reduce_fusion.3) | copy-start | bytes 9220
  427.8 132.9 %copy-start.60 = (f32[768]{0:T(1024)S(1)}, f32[768]{0:T(1024)}, u32[]{:S(2)}) copy-start(f32[768]{0:T(1024)} %get-tuple-element.54) | copy-start | bytes 9220
  427.8 132.9 %copy-start.61 = (f32[768]{0:T(1024)S(1)}, f32[768]{0:T(1024)}, u32[]{:S(2)}) copy-start(f32[768]{0:T(1024)} %get-tuple-element.56) | copy-start | bytes 9220
  427.8 132.9 %copy-start.62 = (f32[3072]{0:T(1024)S(1)}, f32[3072]{0:T(1024)}, u32[]{:S(2)}) copy-start(f32[3072]{0:T(1024)} %get-tuple-element.94) | copy-start | bytes 36868
  427.8 132.9 %copy-start.68 = (f32[768]{0:T(1024)S(1)}, f32[768]{0:T(1024)}, u32[]{:S(2)}) copy-start(f32[768]{0:T(1024)} %get-tuple-element.37) | copy-start | bytes 9220
  427.8 132.9 %copy-start.69 = (f32[768]{0:T(1024)S(1)}, f32[768]{0:T(1024)}, u32[]{:S(2)}) copy-start(f32[768]{0:T(1024)} %get-tuple-element.41) | copy-start | bytes 9220
  560.5 44.1 %copy-start.51 = (f32[48,3072]{1,0:T(8,128)S(1)}, f32[48,3072]{1,0:T(8,128)}, u32[]{:S(2)}) copy-start(f32[48,3072]{1,0:T(8,128)} %get-tuple-element.124) | copy-start | bytes 1769476
  560.5 44.9 %copy-start.50 = (f32[192,768]{1,0:T(8,128)S(1)}, f32[192,768]{1,0:T(8,128)}, u32[]{:S(2)}) copy-start(f32[192,768]{1,0:T(8,128)} %get-tuple-element.126) | copy-start | bytes 1769476
  (63 other events, 168.9 us)
Sparse Core Ops, SparseCore 0:
  216.5 27.1 all-gather.6
  245.2 27.1 all-gather.4
  331.2 26.0 reduce-scatter.8
  371.7 26.1 reduce-scatter.6
